TPU v7x, 1024 devices: a whole 4x8x16 slice. The times are simulated.
1024 devices in a mesh: row: 16 (over z), col: 64 (over y, x, core).
Axes of the slice: x: 4, y: 8, z: 16, core: 2. Of those that a mesh axis runs over, the one named last changes fastest.
Arguments:
- left_tiles: float32 [128, 256, 512], P('row', 'col'), may hold values from 0.005 to 0.05
- left_index: int32 [16, 64, 4], P('row', 'col'), may hold values from 0 to 3, each once within a row
- left_count: int32 [16, 64], P('row', 'col'), may hold values from 1 to 4
- right_tiles: float32 [8192, 8192], P('row', 'col'), may hold values from 0.005 to 0.05
- right_index: int32 [16, 64], P('row', 'col'), may hold values from 0 to 15
Outputs:
- inflated: float32 [128, 8192], P('row', 'col')
All inputs are finite; a program needn't handle non-finite values.
Results may differ from a plain program's by a relative error of at most 0.00005.
Values sent between devices are 32-bit elements; how exact they have to be, the bound alone decides.
A program may use at most 32 MiB of HBM per device.

v0:
```python
import jax
import jax.numpy as jnp
from jax import lax
from jax.sharding import PartitionSpec as P


def body(left_tiles, left_index, left_count, right_tiles, right_index):
    slots = left_tiles.shape[1]
    rows = left_tiles.shape[0]
    width = right_tiles.shape[1]
    tile = right_tiles.shape[0]
    n_rows = lax.axis_size("row")
    n_cols = lax.axis_size("col")
    span = slots * n_cols // n_rows
    alive = jnp.arange(slots) < left_count[0, 0]
    own_ids = jnp.where(alive, left_index.reshape(1, slots), -1)
    own_right = right_tiles.reshape(1, tile, width)
    right_all, right_idx = (
        lax.all_gather(own_right, "row", axis=0, tiled=True),
        lax.all_gather(right_index, "row", axis=0, tiled=True),
    )
    right_ids = (jnp.arange(n_rows) * span + right_idx[:, 0]).astype(jnp.int32)
    strips = lax.all_gather(left_tiles, "col", axis=1, tiled=True)
    ids = lax.all_gather(own_ids, "col", axis=1, tiled=True)
    places = jnp.arange(ids.shape[1])
    left_ids = jnp.where(ids[0] >= 0, places // slots * slots + ids[0], -1).astype(jnp.int32)
    match = (left_ids[:, None] == right_ids[None, :]).astype(jnp.float32)
    chosen = jnp.einsum("qj,bqt->jbt", match, strips, precision=lax.Precision.HIGHEST)
    product = jnp.einsum("jbt,jtx->bx", chosen, right_all, precision=lax.Precision.HIGHEST)
    squared = product * product
    colsum = lax.psum(jnp.sum(squared, axis=0, keepdims=True), "row")
    return rows * n_rows * squared / (colsum + 1e-06)


def solution(mesh):
    return jax.shard_map(
        body,
        mesh=mesh,
        in_specs=(
            P("row", "col", None),
            P("row", "col", None),
            P("row", "col"),
            P("row", "col"),
            P("row", "col"),
        ),
        out_specs=P("row", "col"),
        check_vma=False,
    )
```

profile of v0, /device:TPU:6, one launch (start us, length us, event | category | flops | bytes accessed | tf_op | source)
XLA Modules:
  0.0 239.2 jit_solution(16252066428635964957)
XLA Ops:
  6.5 0.0 all-gather.4.cloned.1.call-start
  6.5 1.5 copy.6
  8.0 0.0 all-gather.4.cloned.1.call-update
  8.1 0.0 all-gather.6.cloned.1.call-start
  8.1 0.7 all-gather.6.cloned.1.call-update
  9.5 1.3 dynamic-slice
  10.8 1.3 dynamic-slice.1
  13.4 0.7 bitcast_dynamic-update-slice_fusion
  14.1 33.1 %all-reduce.1 = s32[16]{0:T(128)S(1)} all-reduce(s32[16]{0:T(128)S(1)} %bitcast_dynamic-update-slice_fusion), channel_id=1, replica_groups=mesh['row'=16,'col'=64] {'row'}, use_global_device_ids=true, to_apply=%add.1 | all-reduce | flops 16 | bytes 128 | tf_op jit(solution)/shard_map/squeeze | solution.py:22
  47.2 0.7 fusion.11
  47.9 19.4 %all-reduce = s32[256]{0:T(256)S(1)} all-reduce(s32[256]{0:T(256)S(1)} %fusion.11), channel_id=1, replica_groups=mesh['row'=16,'col'=64] {'col'}, use_global_device_ids=true, to_apply=%add | all-reduce | flops 256 | bytes 2048 | tf_op jit(solution)/shard_map/squeeze | solution.py:26
  67.3 45.9 %all-gather.4.cloned.1.call-done = f32[8,256,512]{2,0,1:T(8,128)} async-done(((f32[8,4,512]{2,0,1:T(8,128)}), f32[8,256,512]{2,0,1:T(8,128)}) %all-gather.4.cloned.1.call-update) | async-done | bytes 4194320 | tf_op jit(solution)/shard_map/all_gather | solution.py:23
  113.3 5.8 %fusion = f32[16,8,512]{2,0,1:T(8,128)S(1)} fusion(f32[8,256,512]{2,0,1:T(8,128)} %all-gather.4.cloned.1.call-done, s32[16]{0:T(128)S(1)} %multiply_add_fusion, s32[256]{0:T(256)S(1)} %compare_select_fusion), kind=kOutput, calls=%fused_computation | convolution fusion | flops 201330688 | bytes 4457536 | tf_op jit(solution)/shard_map/qj,bqt->jbt/dot_general | solution.py:28
  119.1 78.7 %all-gather.6.cloned.1.call-done = f32[8192,128]{1,0:T(8,128)} async-done(((f32[512,128]{1,0:T(8,128)}), f32[8192,128]{1,0:T(8,128)}) %all-gather.6.cloned.1.call-update) | async-done | bytes 4194320 | tf_op jit(solution)/shard_map/all_gather | solution.py:19
  197.8 4.4 %fusion.12 = (f32[128]{0:T(128)S(1)}, f32[8,128]{1,0:T(8,128)S(1)}) fusion(f32[16,512,128]{2,1,0:T(8,128)} %bitcast.24, f32[16,8,512]{2,0,1:T(8,128)S(1)} %fusion), kind=kOutput, calls=%fused_computation.23 | convolution fusion | flops 100665216 | bytes 4461056 | tf_op jit(solution)/shard_map/jbt,jtx->bx/dot_general | solution.py:29
  202.2 29.6 %psum.7 = f32[1,128]{1,0:T(1,128)S(1)} all-reduce(f32[1,128]{1,0:T(1,128)S(1)} %bitcast.25), channel_id=1, replica_groups=mesh['row'=16,'col'=64] {'row'}, use_global_device_ids=true, to_apply=%region_1.2 | all-reduce | flops 128 | bytes 1024 | tf_op jit(solution)/shard_map/psum | solution.py:31
  231.8 0.6 multiply_divide_fusion
  (5 shorter events, 0.0 us)
Async XLA Ops:
  6.5 106.7 %all-gather.4.cloned.1.call-start = ((), (), s32[]{:S(2)}) async-start(), calls=%async_computation | async-start | bytes 4259840 | tf_op jit(solution)/shard_map/all_gather | solution.py:23
  8.1 189.7 %all-gather.6.cloned.1.call-start = ((), (), s32[]{:S(2)}) async-start(), calls=%async_computation.1 | async-start | bytes 4456448 | tf_op jit(solution)/shard_map/all_gather | solution.py:19
Sparse Core Ops, SparseCore 0:
  11.9 101.3 all-gather.3
  115.9 81.8 all-gather.5
where the time goes:
time: 240 us; the launch traced here: 239 us
  waiting for transfers between devices  125 us (52%)
  blocking collectives  82.1 us (34%)
  between operations  15.4 us (6%)
  matrix products  10.2 us (4%)
  local copies, waits for them, and re-layouts  4.78 us (2%)
    all_gather x1, waiting for transfers between devices, body(): lax.all_gather(own_right, 'row', axis=0, tiled=True)  78.7 us
    all_gather x1, waiting for transfers between devices, body(): strips = lax.all_gather(left_tiles, 'col', axis=1, tiled=True)  45.9 us
    squeeze x1, blocking collectives, body(): right_ids = (jnp.arange(n_rows) * span + right_idx[:, 0]).astype(jnp.int32)  33.1 us
    psum x1, blocking collectives, body(): colsum = lax.psum(jnp.sum(squared, axis=0, keepdims=True), 'row')  29.6 us
    squeeze x1, blocking collectives, body(): ids[0] >= 0  19.4 us
    dot_general x1, matrix products, body(): jnp.einsum('qj,bqt->jbt', match, strips, precision=lax.Precision.HIGHEST)  5.79 us
  transfers between devices with their start and end apart: 2, of which 2 were waited for; matrix products, arithmetic and copies ran while one was open for 4% of the time, Pallas kernels for 0%

commit v1 on v0

v1 whole, which is shorter than its diff:
```python
import jax
import jax.numpy as jnp
from jax import lax
from jax.experimental import pallas as pl
from jax.experimental.pallas import tpu as pltpu
from jax.sharding import PartitionSpec as P

MESH = pl.DeviceIdType.MESH
NR, NC = 16, 64


def wait_for(ref, sem):
    pltpu.make_async_copy(ref, ref, sem).wait()


def kernel(
    left, left_index, left_count, right_hbm, right_index, out,
    right, strips, tiles, picked, panel, own_id, ids, ids_s, part, parts, col, cols,
    sem_right, sem_ids, s1, r1, si, ri, s2, r2, s3, r3, s4, r4,
):
    row, me = lax.axis_index("row"), lax.axis_index("col")
    barrier = pltpu.get_barrier_semaphore()

    def greet(r, c):
        pl.semaphore_signal(barrier, inc=1, device_id=(r, c), device_id_type=MESH)

    chunk, place = me // 16, lax.rem(me, 16)
    source_row = lax.rem(place, 4) * 4 + lax.rem(place // 4 + 3, 4)
    target_row, quarter = me // 4, lax.rem(me, 4)
    target_place = lax.rem(row + 1, 4) * 4 + row // 4
    for q in range(4):
        greet(source_row, row * 4 + q)

    def greet_plane(d, _):
        greet(row, lax.rem(me + d, NC))
        return 0

    def greet_line(d, _):
        greet(lax.rem(row + d, NR), me)
        return 0

    lax.fori_loop(1, NC, greet_plane, 0)
    lax.fori_loop(1, NR, greet_line, 0)
    fetch = pltpu.make_async_copy(right_hbm, right, sem_right)
    fetch.start()

    count = left_count[0, 0]
    for k in range(4):
        slot = [left[:, s, k * 128 : (k + 1) * 128] for s in range(4)]
        for t in range(4):
            total = jnp.zeros((8, 128), jnp.float32)
            for s in range(4):
                hit = jnp.logical_and(left_index[0, 0, s] == t, s < count)
                total = jnp.where(hit, slot[s], total)
            strips[k, t] = total
    own_id[...] = jnp.full((1, 128), right_index[0, 0], jnp.int32)
    pl.semaphore_wait(barrier, 4 + NC - 1 + NR - 1)

    def send_strips(k):
        return pltpu.make_async_remote_copy(
            src_ref=strips.at[k],
            dst_ref=tiles.at[pl.ds(quarter * 4, 4)],
            send_sem=s1,
            recv_sem=r1,
            device_id=(target_row, k * 16 + target_place),
            device_id_type=MESH,
        )

    for k in range(4):
        send_strips(k).start()

    def send_id(d, _):
        pltpu.make_async_remote_copy(
            src_ref=own_id,
            dst_ref=ids.at[me],
            send_sem=si,
            recv_sem=ri,
            device_id=(row, lax.rem(me + d, NC)),
            device_id_type=MESH,
        ).start()
        return 0

    lax.fori_loop(1, NC, send_id, 0)
    ids[me] = own_id[...]
    wait_for(ids.at[pl.ds(0, NC - 1)], ri)
    read = pltpu.make_async_copy(ids, ids_s, sem_ids)
    read.start()
    read.wait()
    wait_for(tiles, r1)

    slot_here = chunk * 16 + source_row

    def send_tile(d, _):
        c = lax.rem(me + d, NC)
        picked[d] = tiles[ids_s[c, 0, 0]]
        pltpu.make_async_remote_copy(
            src_ref=picked.at[d],
            dst_ref=panel.at[slot_here],
            send_sem=s2,
            recv_sem=r2,
            device_id=(row, c),
            device_id_type=MESH,
        ).start()
        return 0

    lax.fori_loop(1, NC, send_tile, 0)
    panel[slot_here] = tiles[ids_s[me, 0, 0]]
    fetch.wait()
    wait_for(panel.at[pl.ds(0, NC - 1)], r2)

    total = jnp.zeros((128, 128), jnp.float32)
    for k in range(4):
        a = panel[pl.ds(k * 16, 16)].reshape(128, 128)
        b = right[pl.ds(k * 128, 128), :]
        total += jnp.dot(a, b, precision=lax.Precision.HIGHEST, preferred_element_type=jnp.float32)
    part[...] = total.reshape(NR, 8, 128)

    def send_part(d, _):
        r = lax.rem(row + d, NR)
        pltpu.make_async_remote_copy(
            src_ref=part.at[r],
            dst_ref=parts.at[row],
            send_sem=s3,
            recv_sem=r3,
            device_id=(r, me),
            device_id_type=MESH,
        ).start()
        return 0

    lax.fori_loop(1, NR, send_part, 0)
    parts[row] = part[row]
    wait_for(parts.at[pl.ds(0, NR - 1)], r3)
    product = jnp.sum(parts[...], axis=0)
    squared = product * product
    col[...] = jnp.sum(squared, axis=0, keepdims=True)

    def send_col(d, _):
        pltpu.make_async_remote_copy(
            src_ref=col,
            dst_ref=cols.at[row],
            send_sem=s4,
            recv_sem=r4,
            device_id=(lax.rem(row + d, NR), me),
            device_id_type=MESH,
        ).start()
        return 0

    lax.fori_loop(1, NR, send_col, 0)
    cols[row] = col[...]
    wait_for(cols.at[pl.ds(0, NR - 1)], r4)
    colsum = jnp.sum(cols[...], axis=0)
    out[...] = 128.0 * squared / (colsum + 1e-06)

    wait_for(strips, s1)
    wait_for(ids.at[pl.ds(0, NC - 1)], si)
    wait_for(picked.at[pl.ds(1, NC - 1)], s2)
    wait_for(part.at[pl.ds(0, NR - 1)], s3)
    wait_for(cols.at[pl.ds(0, NR - 1)], s4)


def body(left_tiles, left_index, left_count, right_tiles, right_index):
    vmem, smem = (pl.BlockSpec(memory_space=m) for m in (pltpu.VMEM, pltpu.SMEM))
    f32, i32 = jnp.float32, jnp.int32
    return pl.pallas_call(
        kernel,
        out_shape=jax.ShapeDtypeStruct((8, 128), f32),
        in_specs=[vmem, smem, smem, pl.BlockSpec(memory_space=pl.ANY), smem],
        out_specs=vmem,
        scratch_shapes=[
            pltpu.VMEM((512, 128), f32),
            pltpu.VMEM((4, 4, 8, 128), f32),
            pltpu.VMEM((16, 8, 128), f32),
            pltpu.VMEM((NC, 8, 128), f32),
            pltpu.VMEM((NC, 8, 128), f32),
            pltpu.VMEM((1, 128), i32),
            pltpu.VMEM((NC, 1, 128), i32),
            pltpu.SMEM((NC, 1, 128), i32),
            pltpu.VMEM((NR, 8, 128), f32),
            pltpu.VMEM((NR, 8, 128), f32),
            pltpu.VMEM((1, 128), f32),
            pltpu.VMEM((NR, 1, 128), f32),
        ]
        + [pltpu.SemaphoreType.DMA] * 12,
        compiler_params=pltpu.CompilerParams(
            collective_id=0, has_side_effects=True, vmem_limit_bytes=56 << 20
        ),
    )(left_tiles, left_index, left_count, right_tiles, right_index)


def solution(mesh):
    return jax.shard_map(
        body,
        mesh=mesh,
        in_specs=(
            P("row", "col", None),
            P("row", "col", None),
            P("row", "col"),
            P("row", "col"),
            P("row", "col"),
        ),
        out_specs=P("row", "col"),
        check_vma=False,
    )
```

time: 240 us -> 67.5 us (0.28)
  the two profiles are of different devices: /device:TPU:6 before, /device:TPU:16 now
where the time goes in v1:
time: 67.5 us; the launch traced here: 67.2 us
  Pallas kernels  64.7 us (96%)
  between operations  1.3 us (2%)
  local copies, waits for them, and re-layouts  1.28 us (2%)
    pallas_call x1, Pallas kernels, body(): pl.pallas_call(kernel, out_shape=jax.ShapeDtypeStruct((8, 128), f32), in_...  64.7 us

profile of v1, /device:TPU:16, one launch (start us, length us, event | category | flops | bytes accessed | tf_op | source)
XLA Modules:
  0.0 67.2 jit_solution(10338937447152633098)
XLA Ops:
  1.3 64.7 %shard_map.55 = f32[8,128]{1,0:T(8,128)} custom-call(f32[8,4,512]{2,1,0:T(4,128)} %left.1, s32[1,1,4]{2,1,0:T(1,128)} %left_index.1, s32[1,1]{1,0:T(1,128)S(6)} %copy.7.left_count, f32[512,128]{1,0:T(8,128)} %right_hbm.1, s32[1,1]{1,0:T(1,128)S(6)} %copy.8.right_index), custom_call_target="tpu_custom_call" | custom-call | tf_op jit(solution)/shard_map/pallas_call | solution.py:164
  66.0 1.3 %copy.9 = f32[8,128]{1,0:T(8,128)} copy(f32[8,128]{1,0:T(8,128)} %shard_map.55) | data formatting | bytes 8192

commit v2 on v1

v2 whole, which is shorter than its diff:
```python
import jax
import jax.numpy as jnp
from jax import lax
from jax.experimental import pallas as pl
from jax.experimental.pallas import tpu as pltpu
from jax.sharding import PartitionSpec as P

MESH = pl.DeviceIdType.MESH
NR, NC = 16, 64


def wait_for(ref, sem):
    pltpu.make_async_copy(ref, ref, sem).wait()


def kernel(
    left_hbm, index_hbm, count_hbm, right_hbm, own_hbm, out,
    left, left_index, left_count, right, right_index,
    strips, staged, tiles, picked, panel, own_id, ids, ids_s, part, near, half, far, result, mine,
    sem_left, sem_int, sem_right, sem_ids, s1, r1, s2, r2, si, ri, s3, r3, s4, r4, s5, r5, s6, r6,
):
    row, me = lax.axis_index("row"), lax.axis_index("col")
    barrier = pltpu.get_barrier_semaphore()

    def greet(r, c):
        pl.semaphore_signal(barrier, inc=1, device_id=(r, c), device_id_type=MESH)

    y, x, core = me // 8, lax.rem(me // 2, 4), lax.rem(me, 2)
    quarter = lax.rem(me, 4)
    offset = lax.rem(y - row // 2 + 8, 8)
    chunk = offset // 2
    source = (1 - x // 2) + 2 * lax.rem(x, 2) + 4 * core + 8 * lax.rem(offset, 2)
    parity = row // 8
    hold_x, hold_core = 2 * (1 - lax.rem(row, 2)) + lax.rem(row // 2, 2), lax.rem(row // 4, 2)

    def greet_line(d, _):
        greet(lax.rem(row + d, NR), me)
        return 0

    def greet_plane(d, _):
        greet(row, lax.rem(me + d, NC))
        return 0

    lax.fori_loop(1, NC, greet_plane, 0)
    for q in range(4):
        greet(source, y * 8 + lax.rem(row, 2) * 4 + q)
    lax.fori_loop(1, NR, greet_line, 0)

    ints = ((index_hbm, left_index), (count_hbm, left_count), (own_hbm, right_index))
    fetch_ints = [pltpu.make_async_copy(a, b, sem_int.at[i]) for i, (a, b) in enumerate(ints)]
    fetch_left = pltpu.make_async_copy(left_hbm, left, sem_left)
    fetch_right = pltpu.make_async_copy(right_hbm, right, sem_right)
    for fetch in fetch_ints:
        fetch.start()
    fetch_left.start()
    fetch_right.start()
    for fetch in fetch_ints:
        fetch.wait()
    fetch_left.wait()

    count = left_count[0, 0]
    for k in range(4):
        slot = [left[:, s, k * 128 : (k + 1) * 128] for s in range(4)]
        for t in range(4):
            total = jnp.zeros((8, 128), jnp.float32)
            for s in range(4):
                hit = jnp.logical_and(left_index[0, 0, s] == t, s < count)
                total = jnp.where(hit, slot[s], total)
            strips[k, t] = total
    own_id[...] = jnp.full((1, 128), right_index[0, 0], jnp.int32)
    pl.semaphore_wait(barrier, NC - 1 + 4 + NR - 1)

    def spread(k):
        return pltpu.make_async_remote_copy(
            src_ref=strips.at[k],
            dst_ref=staged.at[k],
            send_sem=s1.at[k],
            recv_sem=r1.at[k],
            device_id=(row, lax.rem(y + 2 * k + parity, 8) * 8 + lax.rem(me, 8)),
            device_id_type=MESH,
        )

    for k in range(1, 4):
        spread(k).start()
    pl.when(parity == 1)(lambda: spread(0).start())

    @pl.when(parity == 0)
    def _():
        staged[0] = strips[0]

    def send_id(d, _):
        pltpu.make_async_remote_copy(
            src_ref=own_id,
            dst_ref=ids.at[me],
            send_sem=si,
            recv_sem=ri,
            device_id=(row, lax.rem(me + d, NC)),
            device_id_type=MESH,
        ).start()
        return 0

    lax.fori_loop(1, NC, send_id, 0)
    ids[me] = own_id[...]

    def to_plane(k):
        plane = 2 * lax.rem(y - 2 * k - parity + 8, 8) + x // 2
        return pltpu.make_async_remote_copy(
            src_ref=staged.at[k],
            dst_ref=tiles.at[pl.ds(quarter * 4, 4)],
            send_sem=s2,
            recv_sem=r2,
            device_id=(plane, y * 8 + hold_x * 2 + hold_core),
            device_id_type=MESH,
        )

    pl.when(parity == 1)(lambda: spread(0).wait_recv())
    to_plane(0).start()
    for k in (1, 3, 2):
        spread(k).wait_recv()
        to_plane(k).start()
    wait_for(ids.at[pl.ds(0, NC - 1)], ri)
    read = pltpu.make_async_copy(ids, ids_s, sem_ids)
    read.start()
    read.wait()
    wait_for(tiles, r2)

    slot_here = chunk * 16 + source

    def send_tile(d, _):
        c = lax.rem(me + d, NC)
        picked[d] = tiles[ids_s[c, 0, 0]]
        pltpu.make_async_remote_copy(
            src_ref=picked.at[d],
            dst_ref=panel.at[slot_here],
            send_sem=s3,
            recv_sem=r3,
            device_id=(row, c),
            device_id_type=MESH,
        ).start()
        return 0

    lax.fori_loop(1, NC, send_tile, 0)
    panel[slot_here] = tiles[ids_s[me, 0, 0]]
    fetch_right.wait()
    wait_for(panel.at[pl.ds(0, NC - 1)], r3)

    total = jnp.zeros((128, 128), jnp.float32)
    for k in range(4):
        a = panel[pl.ds(k * 16, 16)].reshape(128, 128)
        b = right[pl.ds(k * 128, 128), :]
        total += jnp.dot(a, b, precision=lax.Precision.HIGHEST, preferred_element_type=jnp.float32)
    part[...] = total.reshape(4, 4, 8, 128)

    base, member = row // 4 * 4, lax.rem(row, 4)
    for d in range(1, 4):
        m = lax.rem(member + d, 4)
        pltpu.make_async_remote_copy(
            src_ref=part.at[m],
            dst_ref=near.at[member],
            send_sem=s4,
            recv_sem=r4,
            device_id=(base + m, me),
            device_id_type=MESH,
        ).start()
    near[member] = part[member]
    wait_for(near.at[pl.ds(0, 3)], r4)
    summed = near[0] + near[1] + near[2] + near[3]

    def give(r):
        return pltpu.make_async_remote_copy(
            src_ref=result.at[r],
            dst_ref=mine,
            send_sem=s6,
            recv_sem=r6,
            device_id=(r, me),
            device_id_type=MESH,
        )

    @pl.when(row != 0)
    def _():
        half[...] = summed
        copy = pltpu.make_async_remote_copy(
            src_ref=half,
            dst_ref=far.at[row],
            send_sem=s5,
            recv_sem=r5,
            device_id=(0, me),
            device_id_type=MESH,
        )
        copy.start()
        wait_for(mine, r6)
        out[...] = mine[...]
        copy.wait_send()

    @pl.when(row == 0)
    def _():
        far[0] = summed
        wait_for(far.at[pl.ds(0, NR - 1)], r5)
        product = jnp.sum(far[...].reshape(4, 16, 8, 128), axis=0)
        squared = product * product
        colsum = jnp.sum(jnp.sum(squared, axis=0), axis=0, keepdims=True)
        result[...] = 128.0 * squared / (colsum + 1e-06)[None]
        for r in range(1, NR):
            give(r).start()
        out[...] = result[0]
        wait_for(result.at[pl.ds(0, NR - 1)], s6)

    for k in range(1, 4):
        spread(k).wait_send()
    pl.when(parity == 1)(lambda: spread(0).wait_send())
    wait_for(tiles, s2)
    wait_for(ids.at[pl.ds(0, NC - 1)], si)
    wait_for(picked.at[pl.ds(1, NC - 1)], s3)
    wait_for(near.at[pl.ds(0, 3)], s4)


def body(left_tiles, left_index, left_count, right_tiles, right_index):
    f32, i32 = jnp.float32, jnp.int32
    dma = pltpu.SemaphoreType.DMA
    return pl.pallas_call(
        kernel,
        out_shape=jax.ShapeDtypeStruct((8, 128), f32),
        in_specs=[pl.BlockSpec(memory_space=pltpu.HBM)] * 5,
        out_specs=pl.BlockSpec(memory_space=pltpu.VMEM),
        scratch_shapes=[
            pltpu.VMEM((8, 4, 512), f32),
            pltpu.SMEM((1, 1, 4), i32),
            pltpu.SMEM((1, 1), i32),
            pltpu.VMEM((512, 128), f32),
            pltpu.SMEM((1, 1), i32),
            pltpu.VMEM((4, 4, 8, 128), f32),
            pltpu.VMEM((4, 4, 8, 128), f32),
            pltpu.VMEM((16, 8, 128), f32),
            pltpu.VMEM((NC, 8, 128), f32),
            pltpu.VMEM((NC, 8, 128), f32),
            pltpu.VMEM((1, 128), i32),
            pltpu.VMEM((NC, 1, 128), i32),
            pltpu.SMEM((NC, 1, 128), i32),
            pltpu.VMEM((4, 4, 8, 128), f32),
            pltpu.VMEM((4, 4, 8, 128), f32),
            pltpu.VMEM((4, 8, 128), f32),
            pltpu.VMEM((NR, 4, 8, 128), f32),
            pltpu.VMEM((NR, 8, 128), f32),
            pltpu.VMEM((8, 128), f32),
            dma, dma((3,)), dma, dma, dma((4,)), dma((4,)),
        ]
        + [dma] * 12,
        compiler_params=pltpu.CompilerParams(
            collective_id=0, has_side_effects=True, vmem_limit_bytes=56 << 20
        ),
    )(left_tiles, left_index, left_count, right_tiles, right_index)


def solution(mesh):
    return jax.shard_map(
        body,
        mesh=mesh,
        in_specs=(
            P("row", "col", None),
            P("row", "col", None),
            P("row", "col"),
            P("row", "col"),
            P("row", "col"),
        ),
        out_specs=P("row", "col"),
        check_vma=False,
    )
```

time: 67.5 us -> 59.8 us (0.89)
  the two profiles are of different devices: /device:TPU:16 before, /device:TPU:6 now
where the time goes in v2:
time: 59.8 us; the launch traced here: 59.4 us
  Pallas kernels  56.9 us (95%)
  between operations  1.3 us (2%)
  local copies, waits for them, and re-layouts  1.28 us (2%)
    pallas_call x1, Pallas kernels, body(): pl.pallas_call(kernel, out_shape=jax.ShapeDtypeStruct((8, 128), f32), in_...  56.9 us
    unnamed x1, local copies, waits for them, and re-layouts  1.28 us

profile of v2, /device:TPU:6, one launch (start us, length us, event | category | flops | bytes accessed | tf_op | source)
XLA Modules:
  0.0 59.4 jit_solution(11280754571456520904)
XLA Ops:
  1.3 56.9 %shard_map.55 = f32[8,128]{1,0:T(8,128)} custom-call(f32[8,4,512]{2,1,0:T(4,128)} %left_hbm.1, s32[1,1,4]{2,1,0:T(1,128)} %index_hbm.1, s32[1,1]{1,0:T(1,128)S(6)} %copy.7.count_hbm, f32[512,128]{1,0:T(8,128)} %right_hbm.1, s32[1,1]{1,0:T(1,128)S(6)} %copy.8.own_hbm), custom_call_target="tpu_custom_call" | custom-call | tf_op jit(solution)/shard_map/pallas_call | solution.py:220
  58.2 1.3 %copy.9 = f32[8,128]{1,0:T(8,128)} copy(f32[8,128]{1,0:T(8,128)} %shard_map.55) | data formatting | bytes 8192

commit v3 on v2

--- a/solution.py
+++ b/solution.py
@@ -17,7 +17,7 @@
     left_hbm, index_hbm, count_hbm, right_hbm, own_hbm, out,
     left, left_index, left_count, right, right_index,
     strips, staged, tiles, picked, panel, own_id, ids, ids_s, part, near, half, far, result, mine,
-    sem_left, sem_int, sem_right, sem_ids, s1, r1, s2, r2, si, ri, s3, r3, s4, r4, s5, r5, s6, r6,
+    sem_left, sem_int, sem_right, sem_ids, s1, r1, s2, r2, si, ri, s3, r3, s4, r4, s5, r5, s6, r6, ready, plane_ready, near_ready,
 ):
     row, me = lax.axis_index("row"), lax.axis_index("col")
     barrier = pltpu.get_barrier_semaphore()
@@ -33,18 +33,46 @@
     parity = row // 8
     hold_x, hold_core = 2 * (1 - lax.rem(row, 2)) + lax.rem(row // 2, 2), lax.rem(row // 4, 2)
 
-    def greet_line(d, _):
-        greet(lax.rem(row + d, NR), me)
-        return 0
-
-    def greet_plane(d, _):
-        greet(row, lax.rem(me + d, NC))
-        return 0
-
-    lax.fori_loop(1, NC, greet_plane, 0)
-    for q in range(4):
-        greet(source, y * 8 + lax.rem(row, 2) * 4 + q)
-    lax.fori_loop(1, NR, greet_line, 0)
+    planes = [2 * lax.rem(y - 2 * k - parity + 8, 8) + x // 2 for k in range(4)]
+    above = [(p > row).astype(jnp.int32) for p in planes]
+    below = [(p < row).astype(jnp.int32) for p in planes]
+    n_above = above[0] + above[1] + above[2] + above[3]
+    n_below = below[0] + below[1] + below[2] + below[3]
+    member = lax.rem(row, 4)
+
+    def on_line(d):
+        return lax.rem(y + d, 8) * 8 + lax.rem(me, 8)
+
+    def sender(q):
+        return y * 8 + lax.rem(row, 2) * 4 + q
+
+    def holder(k):
+        return planes[k], y * 8 + hold_x * 2 + hold_core
+
+    for d in range(1, 8):
+        greet(row, on_line(d))
+    for d in range(1, 8):
+        greet(row, y * 8 + lax.rem(me + d, 8))
+
+    @pl.when(source > row)
+    def _():
+        for q in range(4):
+            greet(source, sender(q))
+
+    for k in range(4):
+        pl.when(planes[k] > row)(lambda k=k: greet(*holder(k)))
+    for d in range(1, 4):
+        pl.when(member + d < 4)(lambda d=d: greet(row + d, me))
+
+    @pl.when(row == 0)
+    def _():
+        def greet_line(r, _):
+            greet(r, me)
+            return 0
+
+        lax.fori_loop(4, NR, greet_line, 0)
+
+    expected = 14 + 4 * (source < row).astype(jnp.int32) + n_below + member + (row >= 4).astype(jnp.int32)
 
     ints = ((index_hbm, left_index), (count_hbm, left_count), (own_hbm, right_index))
     fetch_ints = [pltpu.make_async_copy(a, b, sem_int.at[i]) for i, (a, b) in enumerate(ints)]
@@ -68,7 +96,7 @@
                 total = jnp.where(hit, slot[s], total)
             strips[k, t] = total
     own_id[...] = jnp.full((1, 128), right_index[0, 0], jnp.int32)
-    pl.semaphore_wait(barrier, NC - 1 + 4 + NR - 1)
+    pl.semaphore_wait(barrier, expected)
 
     def spread(k):
         return pltpu.make_async_remote_copy(
@@ -76,7 +104,7 @@
             dst_ref=staged.at[k],
             send_sem=s1.at[k],
             recv_sem=r1.at[k],
-            device_id=(row, lax.rem(y + 2 * k + parity, 8) * 8 + lax.rem(me, 8)),
+            device_id=(row, on_line(2 * k + parity)),
             device_id_type=MESH,
         )
 
@@ -87,6 +115,35 @@
     @pl.when(parity == 0)
     def _():
         staged[0] = strips[0]
+
+    def tell(sem, r, c):
+        pl.semaphore_signal(sem, inc=1, device_id=(r, c), device_id_type=MESH)
+
+    @pl.when(source < row)
+    def _():
+        for q in range(4):
+            tell(ready, source, sender(q))
+
+    for d in range(1, 8):
+        tell(plane_ready, row, on_line(d))
+    for d in range(1, 4):
+        pl.when(member >= d)(lambda d=d: tell(near_ready, row - d, me))
+
+    def to_plane(k):
+        return pltpu.make_async_remote_copy(
+            src_ref=staged.at[k],
+            dst_ref=tiles.at[pl.ds(quarter * 4, 4)],
+            send_sem=s2,
+            recv_sem=r2,
+            device_id=holder(k),
+            device_id_type=MESH,
+        )
+
+    pl.when(parity == 1)(lambda: spread(0).wait_recv())
+    pl.when(planes[0] <= row)(lambda: to_plane(0).start())
+    for k in (1, 3, 2):
+        spread(k).wait_recv()
+        pl.when(planes[k] <= row)(lambda k=k: to_plane(k).start())
 
     def send_id(d, _):
         pltpu.make_async_remote_copy(
@@ -99,25 +156,16 @@
         ).start()
         return 0
 
+    pl.semaphore_wait(plane_ready, 7)
     lax.fori_loop(1, NC, send_id, 0)
     ids[me] = own_id[...]
 
-    def to_plane(k):
-        plane = 2 * lax.rem(y - 2 * k - parity + 8, 8) + x // 2
-        return pltpu.make_async_remote_copy(
-            src_ref=staged.at[k],
-            dst_ref=tiles.at[pl.ds(quarter * 4, 4)],
-            send_sem=s2,
-            recv_sem=r2,
-            device_id=(plane, y * 8 + hold_x * 2 + hold_core),
-            device_id_type=MESH,
-        )
-
-    pl.when(parity == 1)(lambda: spread(0).wait_recv())
-    to_plane(0).start()
-    for k in (1, 3, 2):
-        spread(k).wait_recv()
-        to_plane(k).start()
+    @pl.when(n_above > 0)
+    def _():
+        pl.semaphore_wait(ready, n_above)
+        for k in range(4):
+            pl.when(planes[k] > row)(lambda k=k: to_plane(k).start())
+
     wait_for(ids.at[pl.ds(0, NC - 1)], ri)
     read = pltpu.make_async_copy(ids, ids_s, sem_ids)
     read.start()
@@ -149,22 +197,20 @@
         a = panel[pl.ds(k * 16, 16)].reshape(128, 128)
         b = right[pl.ds(k * 128, 128), :]
         total += jnp.dot(a, b, precision=lax.Precision.HIGHEST, preferred_element_type=jnp.float32)
-    part[...] = total.reshape(4, 4, 8, 128)
-
-    base, member = row // 4 * 4, lax.rem(row, 4)
-    for d in range(1, 4):
-        m = lax.rem(member + d, 4)
-        pltpu.make_async_remote_copy(
-            src_ref=part.at[m],
+    part[...] = total.reshape(2, 8, 8, 128)
+
+    group = row // 4
+    first = group * 4 + group // 2 * 2
+
+    def gather_near(h):
+        return pltpu.make_async_remote_copy(
+            src_ref=part.at[h],
             dst_ref=near.at[member],
-            send_sem=s4,
+            send_sem=s4.at[h],
             recv_sem=r4,
-            device_id=(base + m, me),
-            device_id_type=MESH,
-        ).start()
-    near[member] = part[member]
-    wait_for(near.at[pl.ds(0, 3)], r4)
-    summed = near[0] + near[1] + near[2] + near[3]
+            device_id=(first + h, me),
+            device_id_type=MESH,
+        )
 
     def give(r):
         return pltpu.make_async_remote_copy(
@@ -176,26 +222,37 @@
             device_id_type=MESH,
         )
 
+    pl.when(member < 3)(lambda: pl.semaphore_wait(near_ready, 3 - member))
+    for h in range(2):
+        pl.when(row != first + h)(lambda h=h: gather_near(h).start())
+    for h in range(2):
+
+        @pl.when(row == first + h)
+        def _(h=h):
+            near[member] = part[h]
+            wait_for(near.at[pl.ds(0, 3)], r4)
+            half[...] = near[0] + near[1] + near[2] + near[3]
+
+    gather_far = pltpu.make_async_remote_copy(
+        src_ref=half,
+        dst_ref=far.at[group * 2 + row - first],
+        send_sem=s5,
+        recv_sem=r5,
+        device_id=(0, me),
+        device_id_type=MESH,
+    )
+    holds = jnp.logical_and(row != 0, jnp.logical_or(row == first, row == first + 1))
+    pl.when(holds)(lambda: gather_far.start())
+
     @pl.when(row != 0)
     def _():
-        half[...] = summed
-        copy = pltpu.make_async_remote_copy(
-            src_ref=half,
-            dst_ref=far.at[row],
-            send_sem=s5,
-            recv_sem=r5,
-            device_id=(0, me),
-            device_id_type=MESH,
-        )
-        copy.start()
         wait_for(mine, r6)
         out[...] = mine[...]
-        copy.wait_send()
 
     @pl.when(row == 0)
     def _():
-        far[0] = summed
-        wait_for(far.at[pl.ds(0, NR - 1)], r5)
+        far[0] = half[...]
+        wait_for(far.at[pl.ds(0, 7)], r5)
         product = jnp.sum(far[...].reshape(4, 16, 8, 128), axis=0)
         squared = product * product
         colsum = jnp.sum(jnp.sum(squared, axis=0), axis=0, keepdims=True)
@@ -205,13 +262,15 @@
         out[...] = result[0]
         wait_for(result.at[pl.ds(0, NR - 1)], s6)
 
+    pl.when(holds)(lambda: gather_far.wait_send())
+    for h in range(2):
+        pl.when(row != first + h)(lambda h=h: gather_near(h).wait_send())
     for k in range(1, 4):
         spread(k).wait_send()
     pl.when(parity == 1)(lambda: spread(0).wait_send())
     wait_for(tiles, s2)
     wait_for(ids.at[pl.ds(0, NC - 1)], si)
     wait_for(picked.at[pl.ds(1, NC - 1)], s3)
-    wait_for(near.at[pl.ds(0, 3)], s4)
 
 
 def body(left_tiles, left_index, left_count, right_tiles, right_index):
@@ -236,15 +295,18 @@
             pltpu.VMEM((1, 128), i32),
             pltpu.VMEM((NC, 1, 128), i32),
             pltpu.SMEM((NC, 1, 128), i32),
-            pltpu.VMEM((4, 4, 8, 128), f32),
-            pltpu.VMEM((4, 4, 8, 128), f32),
-            pltpu.VMEM((4, 8, 128), f32),
-            pltpu.VMEM((NR, 4, 8, 128), f32),
+            pltpu.VMEM((2, 8, 8, 128), f32),
+            pltpu.VMEM((4, 8, 8, 128), f32),
+            pltpu.VMEM((8, 8, 128), f32),
+            pltpu.VMEM((8, 8, 8, 128), f32),
             pltpu.VMEM((NR, 8, 128), f32),
             pltpu.VMEM((8, 128), f32),
             dma, dma((3,)), dma, dma, dma((4,)), dma((4,)),
         ]
-        + [dma] * 12,
+        + [dma] * 6
+        + [dma((2,))]
+        + [dma] * 5
+        + [pltpu.SemaphoreType.REGULAR] * 3,
         compiler_params=pltpu.CompilerParams(
             collective_id=0, has_side_effects=True, vmem_limit_bytes=56 << 20
         ),

time: 59.8 us -> 57.9 us (0.968)
  Pallas kernels: 56.9 us -> 55 us
    pallas_call x1, Pallas kernels: 56.9 us -> 55 us  [body(): pl.pallas_call(kernel, out_shape=jax.ShapeDtypeStruct((8, 128), f32), in_...]
where the time goes in v3:
time: 57.9 us; the launch traced here: 57.6 us
  Pallas kernels  55 us (95%)
  between operations  1.3 us (2%)
  local copies, waits for them, and re-layouts  1.28 us (2%)
    pallas_call x1, Pallas kernels, body(): pl.pallas_call(kernel, out_shape=jax.ShapeDtypeStruct((8, 128), f32), in_...  55 us
    unnamed x1, local copies, waits for them, and re-layouts  1.28 us

profile of v3, /device:TPU:6, one launch (start us, length us, event | category | flops | bytes accessed | tf_op | source)
XLA Modules:
  0.0 57.6 jit_solution(344174285080593298)
XLA Ops:
  1.3 55.0 %shard_map.55 = f32[8,128]{1,0:T(8,128)} custom-call(f32[8,4,512]{2,1,0:T(4,128)} %left_hbm.1, s32[1,1,4]{2,1,0:T(1,128)} %index_hbm.1, s32[1,1]{1,0:T(1,128)S(6)} %copy.7.count_hbm, f32[512,128]{1,0:T(8,128)} %right_hbm.1, s32[1,1]{1,0:T(1,128)S(6)} %copy.8.own_hbm), custom_call_target="tpu_custom_call" | custom-call | tf_op jit(solution)/shard_map/pallas_call | solution.py:279
  56.3 1.3 %copy.9 = f32[8,128]{1,0:T(8,128)} copy(f32[8,128]{1,0:T(8,128)} %shard_map.55) | data formatting | bytes 8192

commit v4 on v3

--- a/solution.py
+++ b/solution.py
@@ -17,7 +17,7 @@
     left_hbm, index_hbm, count_hbm, right_hbm, own_hbm, out,
     left, left_index, left_count, right, right_index,
     strips, staged, tiles, picked, panel, own_id, ids, ids_s, part, near, half, far, result, mine,
-    sem_left, sem_int, sem_right, sem_ids, s1, r1, s2, r2, si, ri, s3, r3, s4, r4, s5, r5, s6, r6, ready, plane_ready, near_ready,
+    sem_left, sem_int, sem_right, sem_ids, s1, r1, s2, r2, si, ri, sj, rj, s3, r3, s4, r4, s5, r5, s6, r6, ready, plane_ready, near_ready,
 ):
     row, me = lax.axis_index("row"), lax.axis_index("col")
     barrier = pltpu.get_barrier_semaphore()
@@ -29,9 +29,9 @@
     quarter = lax.rem(me, 4)
     offset = lax.rem(y - row // 2 + 8, 8)
     chunk = offset // 2
-    source = (1 - x // 2) + 2 * lax.rem(x, 2) + 4 * core + 8 * lax.rem(offset, 2)
+    source = x // 2 + 2 * lax.rem(x, 2) + 4 * core + 8 * lax.rem(offset, 2)
     parity = row // 8
-    hold_x, hold_core = 2 * (1 - lax.rem(row, 2)) + lax.rem(row // 2, 2), lax.rem(row // 4, 2)
+    hold_x, hold_core = 2 * lax.rem(row, 2) + lax.rem(row // 2, 2), lax.rem(row // 4, 2)
 
     planes = [2 * lax.rem(y - 2 * k - parity + 8, 8) + x // 2 for k in range(4)]
     above = [(p > row).astype(jnp.int32) for p in planes]
@@ -108,6 +108,14 @@
             device_id_type=MESH,
         )
 
+    def tell(sem, r, c):
+        pl.semaphore_signal(sem, inc=1, device_id=(r, c), device_id_type=MESH)
+
+    @pl.when(source < row)
+    def _():
+        for q in range(4):
+            tell(ready, source, sender(q))
+
     for k in range(1, 4):
         spread(k).start()
     pl.when(parity == 1)(lambda: spread(0).start())
@@ -116,14 +124,6 @@
     def _():
         staged[0] = strips[0]
 
-    def tell(sem, r, c):
-        pl.semaphore_signal(sem, inc=1, device_id=(r, c), device_id_type=MESH)
-
-    @pl.when(source < row)
-    def _():
-        for q in range(4):
-            tell(ready, source, sender(q))
-
     for d in range(1, 8):
         tell(plane_ready, row, on_line(d))
     for d in range(1, 4):
@@ -133,32 +133,54 @@
         return pltpu.make_async_remote_copy(
             src_ref=staged.at[k],
             dst_ref=tiles.at[pl.ds(quarter * 4, 4)],
-            send_sem=s2,
+            send_sem=s2.at[k],
             recv_sem=r2,
             device_id=holder(k),
             device_id_type=MESH,
         )
 
+    here = jnp.logical_and(hold_x == x, hold_core == core)
+    kept = [jnp.logical_and(here, planes[k] == row) for k in range(4)]
+    sent = [jnp.logical_not(keep) for keep in kept]
+
+    def keep_here(k):
+        return pltpu.make_async_copy(staged.at[k], tiles.at[pl.ds(quarter * 4, 4)], r2)
+
+    def pass_on(k):
+        pl.when(jnp.logical_and(sent[k], planes[k] <= row))(lambda: to_plane(k).start())
+        pl.when(kept[k])(lambda: keep_here(k).start())
+
+    def send_id(d):
+        return pltpu.make_async_remote_copy(
+            src_ref=own_id,
+            dst_ref=ids.at[y, lax.rem(me, 8)],
+            send_sem=si,
+            recv_sem=ri,
+            device_id=(row, y * 8 + lax.rem(me + d, 8)),
+            device_id_type=MESH,
+        )
+
+    def send_ids(d):
+        return pltpu.make_async_remote_copy(
+            src_ref=ids.at[y],
+            dst_ref=ids.at[y],
+            send_sem=sj,
+            recv_sem=rj,
+            device_id=(row, on_line(d)),
+            device_id_type=MESH,
+        )
+
+    for d in range(1, 8):
+        send_id(d).start()
+    ids[y, lax.rem(me, 8)] = own_id[...]
     pl.when(parity == 1)(lambda: spread(0).wait_recv())
-    pl.when(planes[0] <= row)(lambda: to_plane(0).start())
+    pass_on(0)
+    wait_for(ids.at[0, pl.ds(0, 7)], ri)
+    for d in range(1, 8):
+        send_ids(d).start()
     for k in (1, 3, 2):
         spread(k).wait_recv()
-        pl.when(planes[k] <= row)(lambda k=k: to_plane(k).start())
-
-    def send_id(d, _):
-        pltpu.make_async_remote_copy(
-            src_ref=own_id,
-            dst_ref=ids.at[me],
-            send_sem=si,
-            recv_sem=ri,
-            device_id=(row, lax.rem(me + d, NC)),
-            device_id_type=MESH,
-        ).start()
-        return 0
-
-    pl.semaphore_wait(plane_ready, 7)
-    lax.fori_loop(1, NC, send_id, 0)
-    ids[me] = own_id[...]
+        pass_on(k)
 
     @pl.when(n_above > 0)
     def _():
@@ -166,38 +188,36 @@
         for k in range(4):
             pl.when(planes[k] > row)(lambda k=k: to_plane(k).start())
 
-    wait_for(ids.at[pl.ds(0, NC - 1)], ri)
+    wait_for(ids.at[pl.ds(0, 7)], rj)
     read = pltpu.make_async_copy(ids, ids_s, sem_ids)
     read.start()
     read.wait()
     wait_for(tiles, r2)
+    pl.semaphore_wait(plane_ready, 7)
 
     slot_here = chunk * 16 + source
 
-    def send_tile(d, _):
-        c = lax.rem(me + d, NC)
-        picked[d] = tiles[ids_s[c, 0, 0]]
+    def send_tile(c, d):
+        picked[d] = tiles[ids_s[c // 8, lax.rem(c, 8), 0, 0]]
         pltpu.make_async_remote_copy(
             src_ref=picked.at[d],
             dst_ref=panel.at[slot_here],
             send_sem=s3,
-            recv_sem=r3,
+            recv_sem=r3.at[source // 8],
             device_id=(row, c),
             device_id_type=MESH,
         ).start()
-        return 0
-
-    lax.fori_loop(1, NC, send_tile, 0)
-    panel[slot_here] = tiles[ids_s[me, 0, 0]]
+
+    for n, d in enumerate((4, 3, 5, 2, 6, 1, 7, 0)):
+
+        def send_group(i, _, n=n, d=d):
+            send_tile(lax.rem(y + d, 8) * 8 + lax.rem(me + i, 8), (7 - n) * 8 + i)
+            return 0
+
+        lax.fori_loop(0 if d else 1, 8, send_group, 0)
+
+    panel[slot_here] = tiles[ids_s[y, lax.rem(me, 8), 0, 0]]
     fetch_right.wait()
-    wait_for(panel.at[pl.ds(0, NC - 1)], r3)
-
-    total = jnp.zeros((128, 128), jnp.float32)
-    for k in range(4):
-        a = panel[pl.ds(k * 16, 16)].reshape(128, 128)
-        b = right[pl.ds(k * 128, 128), :]
-        total += jnp.dot(a, b, precision=lax.Precision.HIGHEST, preferred_element_type=jnp.float32)
-    part[...] = total.reshape(2, 8, 8, 128)
 
     group = row // 4
     first = group * 4 + group // 2 * 2
@@ -222,14 +242,29 @@
             device_id_type=MESH,
         )
 
+    def multiply(h):
+        pl.when(source // 8 == h)(lambda: wait_for(panel.at[pl.ds(0, 31)], r3.at[h]))
+        pl.when(source // 8 != h)(lambda: wait_for(panel.at[pl.ds(0, 32)], r3.at[h]))
+        total = jnp.zeros((64, 128), jnp.float32)
+        for k in range(4):
+            a = panel[pl.ds(k * 16 + h * 8, 8)].reshape(64, 128)
+            b = right[pl.ds(k * 128, 128), :]
+            total += jnp.dot(a, b, precision=lax.Precision.HIGHEST, preferred_element_type=jnp.float32)
+        part[h] = total.reshape(8, 8, 128)
+        pl.when(row != first + h)(lambda: gather_near(h).start())
+
+        @pl.when(row == first + h)
+        def _():
+            near[member] = part[h]
+
     pl.when(member < 3)(lambda: pl.semaphore_wait(near_ready, 3 - member))
-    for h in range(2):
-        pl.when(row != first + h)(lambda h=h: gather_near(h).start())
+    own_half = row // 8
+    multiply(own_half)
+    multiply(1 - own_half)
     for h in range(2):
 
         @pl.when(row == first + h)
         def _(h=h):
-            near[member] = part[h]
             wait_for(near.at[pl.ds(0, 3)], r4)
             half[...] = near[0] + near[1] + near[2] + near[3]
 
@@ -256,7 +291,7 @@
         product = jnp.sum(far[...].reshape(4, 16, 8, 128), axis=0)
         squared = product * product
         colsum = jnp.sum(jnp.sum(squared, axis=0), axis=0, keepdims=True)
-        result[...] = 128.0 * squared / (colsum + 1e-06)[None]
+        result[...] = squared * (128.0 / (colsum + 1e-06))[None]
         for r in range(1, NR):
             give(r).start()
         out[...] = result[0]
@@ -268,8 +303,10 @@
     for k in range(1, 4):
         spread(k).wait_send()
     pl.when(parity == 1)(lambda: spread(0).wait_send())
-    wait_for(tiles, s2)
-    wait_for(ids.at[pl.ds(0, NC - 1)], si)
+    for k in range(4):
+        pl.when(sent[k])(lambda k=k: to_plane(k).wait_send())
+    wait_for(ids.at[0, pl.ds(0, 7)], si)
+    wait_for(ids.at[pl.ds(0, 7)], sj)
     wait_for(picked.at[pl.ds(1, NC - 1)], s3)
 
 
@@ -293,18 +330,18 @@
             pltpu.VMEM((NC, 8, 128), f32),
             pltpu.VMEM((NC, 8, 128), f32),
             pltpu.VMEM((1, 128), i32),
-            pltpu.VMEM((NC, 1, 128), i32),
-            pltpu.SMEM((NC, 1, 128), i32),
+            pltpu.VMEM((8, 8, 1, 128), i32),
+            pltpu.SMEM((8, 8, 1, 128), i32),
             pltpu.VMEM((2, 8, 8, 128), f32),
             pltpu.VMEM((4, 8, 8, 128), f32),
             pltpu.VMEM((8, 8, 128), f32),
             pltpu.VMEM((8, 8, 8, 128), f32),
             pltpu.VMEM((NR, 8, 128), f32),
             pltpu.VMEM((8, 128), f32),
-            dma, dma((3,)), dma, dma, dma((4,)), dma((4,)),
+            dma, dma((3,)), dma, dma, dma((4,)), dma((4,)), dma((4,)),
         ]
         + [dma] * 6
-        + [dma((2,))]
+        + [dma((2,)), dma((2,))]
         + [dma] * 5
         + [pltpu.SemaphoreType.REGULAR] * 3,
         compiler_params=pltpu.CompilerParams(

time: 57.9 us -> 56.7 us (0.979)
  Pallas kernels: 55 us -> 54 us
    pallas_call x1, Pallas kernels: 55 us -> 54 us  [body(): pl.pallas_call(kernel, out_shape=jax.ShapeDtypeStruct((8, 128), f32), in_...]
where the time goes in v4:
time: 56.7 us; the launch traced here: 56.5 us
  Pallas kernels  54 us (95%)
  between operations  1.3 us (2%)
  local copies, waits for them, and re-layouts  1.28 us (2%)
    pallas_call x1, Pallas kernels, body(): pl.pallas_call(kernel, out_shape=jax.ShapeDtypeStruct((8, 128), f32), in_...  54 us
    unnamed x1, local copies, waits for them, and re-layouts  1.28 us

profile of v4, /device:TPU:6, one launch (start us, length us, event | category | flops | bytes accessed | tf_op | source)
XLA Modules:
  0.0 56.5 jit_solution(13966654006133795271)
XLA Ops:
  1.3 54.0 %shard_map.55 = f32[8,128]{1,0:T(8,128)} custom-call(f32[8,4,512]{2,1,0:T(4,128)} %left_hbm.1, s32[1,1,4]{2,1,0:T(1,128)} %index_hbm.1, s32[1,1]{1,0:T(1,128)S(6)} %copy.7.count_hbm, f32[512,128]{1,0:T(8,128)} %right_hbm.1, s32[1,1]{1,0:T(1,128)S(6)} %copy.8.own_hbm), custom_call_target="tpu_custom_call" | custom-call | tf_op jit(solution)/shard_map/pallas_call | solution.py:316
  55.3 1.3 %copy.9 = f32[8,128]{1,0:T(8,128)} copy(f32[8,128]{1,0:T(8,128)} %shard_map.55) | data formatting | bytes 8192

commit v5 on v4

--- a/solution.py
+++ b/solution.py
@@ -208,13 +208,15 @@
             device_id_type=MESH,
         ).start()
 
-    for n, d in enumerate((4, 3, 5, 2, 6, 1, 7, 0)):
-
-        def send_group(i, _, n=n, d=d):
-            send_tile(lax.rem(y + d, 8) * 8 + lax.rem(me + i, 8), (7 - n) * 8 + i)
+    for n in range(16):
+        to_core, d = n // 8, (4, 3, 5, 2, 6, 1, 7, 0)[n % 8]
+
+        def send_group(i, _, n=n, to_core=to_core, d=d):
+            c = lax.rem(y + d, 8) * 8 + 2 * lax.rem(x + i, 4) + to_core
+            pl.when(c != me)(lambda: send_tile(c, n * 4 + i))
             return 0
 
-        lax.fori_loop(0 if d else 1, 8, send_group, 0)
+        lax.fori_loop(0, 4, send_group, 0)
 
     panel[slot_here] = tiles[ids_s[y, lax.rem(me, 8), 0, 0]]
     fetch_right.wait()

time: 56.7 us -> 56 us (0.988)
  Pallas kernels: 54 us -> 53.2 us
    pallas_call x1, Pallas kernels: 54 us -> 53.2 us  [body(): pl.pallas_call(kernel, out_shape=jax.ShapeDtypeStruct((8, 128), f32), in_...]
where the time goes in v5:
time: 56 us; the launch traced here: 55.8 us
  Pallas kernels  53.2 us (95%)
  between operations  1.3 us (2%)
  local copies, waits for them, and re-layouts  1.28 us (2%)
    pallas_call x1, Pallas kernels, body(): pl.pallas_call(kernel, out_shape=jax.ShapeDtypeStruct((8, 128), f32), in_...  53.2 us
    unnamed x1, local copies, waits for them, and re-layouts  1.28 us

profile of v5, /device:TPU:6, one launch (start us, length us, event | category | flops | bytes accessed | tf_op | source)
XLA Modules:
  0.0 55.8 jit_solution(11898354780083971690)
XLA Ops:
  1.3 53.2 %shard_map.55 = f32[8,128]{1,0:T(8,128)} custom-call(f32[8,4,512]{2,1,0:T(4,128)} %left_hbm.1, s32[1,1,4]{2,1,0:T(1,128)} %index_hbm.1, s32[1,1]{1,0:T(1,128)S(6)} %copy.7.count_hbm, f32[512,128]{1,0:T(8,128)} %right_hbm.1, s32[1,1]{1,0:T(1,128)S(6)} %copy.8.own_hbm), custom_call_target="tpu_custom_call" | custom-call | tf_op jit(solution)/shard_map/pallas_call | solution.py:318
  54.5 1.3 %copy.9 = f32[8,128]{1,0:T(8,128)} copy(f32[8,128]{1,0:T(8,128)} %shard_map.55) | data formatting | bytes 8192

commit v6 on v5

--- a/solution.py
+++ b/solution.py
@@ -25,55 +25,6 @@
     def greet(r, c):
         pl.semaphore_signal(barrier, inc=1, device_id=(r, c), device_id_type=MESH)
 
-    y, x, core = me // 8, lax.rem(me // 2, 4), lax.rem(me, 2)
-    quarter = lax.rem(me, 4)
-    offset = lax.rem(y - row // 2 + 8, 8)
-    chunk = offset // 2
-    source = x // 2 + 2 * lax.rem(x, 2) + 4 * core + 8 * lax.rem(offset, 2)
-    parity = row // 8
-    hold_x, hold_core = 2 * lax.rem(row, 2) + lax.rem(row // 2, 2), lax.rem(row // 4, 2)
-
-    planes = [2 * lax.rem(y - 2 * k - parity + 8, 8) + x // 2 for k in range(4)]
-    above = [(p > row).astype(jnp.int32) for p in planes]
-    below = [(p < row).astype(jnp.int32) for p in planes]
-    n_above = above[0] + above[1] + above[2] + above[3]
-    n_below = below[0] + below[1] + below[2] + below[3]
-    member = lax.rem(row, 4)
-
-    def on_line(d):
-        return lax.rem(y + d, 8) * 8 + lax.rem(me, 8)
-
-    def sender(q):
-        return y * 8 + lax.rem(row, 2) * 4 + q
-
-    def holder(k):
-        return planes[k], y * 8 + hold_x * 2 + hold_core
-
-    for d in range(1, 8):
-        greet(row, on_line(d))
-    for d in range(1, 8):
-        greet(row, y * 8 + lax.rem(me + d, 8))
-
-    @pl.when(source > row)
-    def _():
-        for q in range(4):
-            greet(source, sender(q))
-
-    for k in range(4):
-        pl.when(planes[k] > row)(lambda k=k: greet(*holder(k)))
-    for d in range(1, 4):
-        pl.when(member + d < 4)(lambda d=d: greet(row + d, me))
-
-    @pl.when(row == 0)
-    def _():
-        def greet_line(r, _):
-            greet(r, me)
-            return 0
-
-        lax.fori_loop(4, NR, greet_line, 0)
-
-    expected = 14 + 4 * (source < row).astype(jnp.int32) + n_below + member + (row >= 4).astype(jnp.int32)
-
     ints = ((index_hbm, left_index), (count_hbm, left_count), (own_hbm, right_index))
     fetch_ints = [pltpu.make_async_copy(a, b, sem_int.at[i]) for i, (a, b) in enumerate(ints)]
     fetch_left = pltpu.make_async_copy(left_hbm, left, sem_left)
@@ -82,6 +33,56 @@
         fetch.start()
     fetch_left.start()
     fetch_right.start()
+
+    y, x, core = me // 8, lax.rem(me // 2, 4), lax.rem(me, 2)
+    quarter = lax.rem(me, 4)
+    offset = lax.rem(y - row // 2 + 8, 8)
+    chunk = offset // 2
+    source = x // 2 + 2 * lax.rem(x, 2) + 4 * core + 8 * lax.rem(offset, 2)
+    parity = row // 8
+    hold_x, hold_core = 2 * lax.rem(row, 2) + lax.rem(row // 2, 2), lax.rem(row // 4, 2)
+
+    planes = [2 * lax.rem(y - 2 * k - parity + 8, 8) + x // 2 for k in range(4)]
+    above = [(p > row).astype(jnp.int32) for p in planes]
+    below = [(p < row).astype(jnp.int32) for p in planes]
+    n_above = above[0] + above[1] + above[2] + above[3]
+    n_below = below[0] + below[1] + below[2] + below[3]
+    member = lax.rem(row, 4)
+
+    def on_line(d):
+        return lax.rem(y + d, 8) * 8 + lax.rem(me, 8)
+
+    def sender(q):
+        return y * 8 + lax.rem(row, 2) * 4 + q
+
+    def holder(k):
+        return planes[k], y * 8 + hold_x * 2 + hold_core
+
+    for d in range(1, 8):
+        greet(row, on_line(d))
+    for d in range(1, 8):
+        greet(row, y * 8 + lax.rem(me + d, 8))
+
+    @pl.when(source > row)
+    def _():
+        for q in range(4):
+            greet(source, sender(q))
+
+    for k in range(4):
+        pl.when(planes[k] > row)(lambda k=k: greet(*holder(k)))
+    for d in range(1, 4):
+        pl.when(member + d < 4)(lambda d=d: greet(row + d, me))
+
+    @pl.when(row == 0)
+    def _():
+        def greet_line(r, _):
+            greet(r, me)
+            return 0
+
+        lax.fori_loop(4, NR, greet_line, 0)
+
+    expected = 14 + 4 * (source < row).astype(jnp.int32) + n_below + member + (row >= 4).astype(jnp.int32)
+
     for fetch in fetch_ints:
         fetch.wait()
     fetch_left.wait()
@@ -247,11 +248,8 @@
     def multiply(h):
         pl.when(source // 8 == h)(lambda: wait_for(panel.at[pl.ds(0, 31)], r3.at[h]))
         pl.when(source // 8 != h)(lambda: wait_for(panel.at[pl.ds(0, 32)], r3.at[h]))
-        total = jnp.zeros((64, 128), jnp.float32)
-        for k in range(4):
-            a = panel[pl.ds(k * 16 + h * 8, 8)].reshape(64, 128)
-            b = right[pl.ds(k * 128, 128), :]
-            total += jnp.dot(a, b, precision=lax.Precision.HIGHEST, preferred_element_type=jnp.float32)
+        a = jnp.concatenate([panel[pl.ds(k * 16 + h * 8, 8)].reshape(64, 128) for k in range(4)], axis=1)
+        total = jnp.dot(a, right[...], precision=lax.Precision.HIGHEST, preferred_element_type=jnp.float32)
         part[h] = total.reshape(8, 8, 128)
         pl.when(row != first + h)(lambda: gather_near(h).start())
 
@@ -347,7 +345,7 @@
         + [dma] * 5
         + [pltpu.SemaphoreType.REGULAR] * 3,
         compiler_params=pltpu.CompilerParams(
-            collective_id=0, has_side_effects=True, vmem_limit_bytes=56 << 20
+            collective_id=0, has_side_effects=True, vmem_limit_bytes=55168 << 10
         ),
     )(left_tiles, left_index, left_count, right_tiles, right_index)
 

time: 56 us -> 54.5 us (0.973)
  Pallas kernels: 53.2 us -> 52.4 us
  local copies, waits for them, and re-layouts: 1.28 us -> 0.6 us
    pallas_call x1, Pallas kernels: 53.2 us -> 52.4 us  [body(): pl.pallas_call(kernel, out_shape=jax.ShapeDtypeStruct((8, 128), f32), in_...]
    unnamed x1 -> x3, local copies, waits for them, and re-layouts: 1.28 us -> 0.6 us
where the time goes in v6:
time: 54.5 us; the launch traced here: 54.3 us
  Pallas kernels  52.4 us (96%)
  between operations  1.33 us (2%)
  local copies, waits for them, and re-layouts  0.6 us (1%)
    pallas_call x1, Pallas kernels, body(): pl.pallas_call(kernel, out_shape=jax.ShapeDtypeStruct((8, 128), f32), in_...  52.4 us

profile of v6, /device:TPU:6, one launch (start us, length us, event | category | flops | bytes accessed | tf_op | source)
XLA Modules:
  0.0 54.3 jit_solution(14915866938302688335)
XLA Ops:
  0.7 0.0 copy-start
  1.3 0.0 copy-done
  1.3 52.4 %shard_map.55 = f32[8,128]{1,0:T(8,128)S(1)} custom-call(f32[8,4,512]{2,1,0:T(4,128)} %left_hbm.1, s32[1,1,4]{2,1,0:T(1,128)S(1)} %copy-done, s32[1,1]{1,0:T(1,128)S(6)} %copy.7.count_hbm, f32[512,128]{1,0:T(8,128)} %right_hbm.1, s32[1,1]{1,0:T(1,128)S(6)} %copy.8.own_hbm), custom_call_target="tpu_custom_call" | custom-call | tf_op jit(solution)/shard_map/pallas_call | solution.py:316
  53.7 0.6 %copy.9 = f32[8,128]{1,0:T(8,128)} copy(f32[8,128]{1,0:T(8,128)S(1)} %shard_map.55) | data formatting | bytes 8192
Async XLA Ops:
  0.7 0.7 %copy-start = (s32[1,1,4]{2,1,0:T(1,128)S(1)}, s32[1,1,4]{2,1,0:T(1,128)}, u32[]{:S(2)}) copy-start(s32[1,1,4]{2,1,0:T(1,128)} %index_hbm.1) | copy-start | bytes 52

commit v7 on v6

--- a/solution.py
+++ b/solution.py
@@ -214,7 +214,10 @@
 
         def send_group(i, _, n=n, to_core=to_core, d=d):
             c = lax.rem(y + d, 8) * 8 + 2 * lax.rem(x + i, 4) + to_core
-            pl.when(c != me)(lambda: send_tile(c, n * 4 + i))
+            if d == 0:
+                pl.when(c != me)(lambda: send_tile(c, n * 4 + i))
+            else:
+                send_tile(c, n * 4 + i)
             return 0
 
         lax.fori_loop(0, 4, send_group, 0)

time: 54.5 us -> 54.5 us (level)
  no operation moved by 1% of the time
where the time goes in v7:
time: 54.5 us; the launch traced here: 54.2 us
  Pallas kernels  52.3 us (96%)
  between operations  1.33 us (2%)
  local copies, waits for them, and re-layouts  0.6 us (1%)
    pallas_call x1, Pallas kernels, body(): pl.pallas_call(kernel, out_shape=jax.ShapeDtypeStruct((8, 128), f32), in_...  52.3 us

profile of v7, /device:TPU:6, one launch (start us, length us, event | category | flops | bytes accessed | tf_op | source)
XLA Modules:
  0.0 54.2 jit_solution(12192286528208652959)
XLA Ops:
  0.7 0.0 copy-start
  1.3 0.0 copy-done
  1.3 52.3 %shard_map.55 = f32[8,128]{1,0:T(8,128)S(1)} custom-call(f32[8,4,512]{2,1,0:T(4,128)} %left_hbm.1, s32[1,1,4]{2,1,0:T(1,128)S(1)} %copy-done, s32[1,1]{1,0:T(1,128)S(6)} %copy.7.count_hbm, f32[512,128]{1,0:T(8,128)} %right_hbm.1, s32[1,1]{1,0:T(1,128)S(6)} %copy.8.own_hbm), custom_call_target="tpu_custom_call" | custom-call | tf_op jit(solution)/shard_map/pallas_call | solution.py:319
  53.6 0.6 %copy.9 = f32[8,128]{1,0:T(8,128)} copy(f32[8,128]{1,0:T(8,128)S(1)} %shard_map.55) | data formatting | bytes 8192
Async XLA Ops:
  0.7 0.7 %copy-start = (s32[1,1,4]{2,1,0:T(1,128)S(1)}, s32[1,1,4]{2,1,0:T(1,128)}, u32[]{:S(2)}) copy-start(s32[1,1,4]{2,1,0:T(1,128)} %index_hbm.1) | copy-start | bytes 52
